TPU v7x, 32 devices: a whole 2x2x4 slice. The times are simulated.
32 devices in a mesh: dp: 8 (over y, x, core), tensor: 4 (over z).
Axes of the slice: x: 2, y: 2, z: 4, core: 2. Of those that a mesh axis runs over, the one named last changes fastest.
Arguments:
- tokens: bfloat16 [512, 4096], P(('dp', 'tensor')), parts along dimension 0, may hold values from -6 to 6
- gate_act: bfloat16 [512, 5120], P('dp', 'tensor'), parts along dimension 0, may hold values from -6 to 6
- up_act: bfloat16 [512, 5120], P('dp', 'tensor'), parts along dimension 0, may hold values from -6 to 6
- down_weight: bfloat16 [5120, 4096], P('tensor'), may hold values from -0.078125 to 0.078125
- norm_gain: float32 [4096], replicated, may hold values from 0.25 to 1.75
Outputs:
- residual_out: bfloat16 [512, 4096], P(('dp', 'tensor')), parts along dimension 0
- next_rows: bfloat16 [512, 4096], P('dp'), parts along dimension 0
- next_scale: float32 [512], P('dp'), parts along dimension 0
There are 8 independent parts, one for each index of `dp`. A program takes and returns all parts, laid end to end along the dimension named above; an argument that names none is the same for every part. Nothing has to cross between parts.
All inputs are finite; a program needn't handle non-finite values. Where the computation divides by a largest or mean magnitude, that divisor is 1e-20 or more.
Results may differ from a plain program's by a relative error of at most 0.009.
Values may be sent and summed in bfloat16 or wider, within the bound.
No kernel may reach another device: no remote copies, remote signals or barrier semaphores. Data moves between devices by JAX's collectives and lax.ppermute only.
A program may use at most 64 MiB of HBM per device.

v0:
```python
import jax
import jax.numpy as jnp
from jax import lax
from jax.sharding import PartitionSpec as P


def body(tokens, gate_act, up_act, down_weight, norm_gain):
    hidden = (jax.nn.silu(gate_act.astype(jnp.float32)) * up_act.astype(jnp.float32)).astype(
        jnp.bfloat16
    )
    product = jnp.dot(hidden, down_weight, preferred_element_type=jnp.float32)
    summed = lax.psum_scatter(
        product.astype(jnp.bfloat16), "tensor", scatter_dimension=0, tiled=True
    ).astype(jnp.float32)
    residual = tokens.astype(jnp.float32) + summed
    mean_square = jnp.mean(residual * residual, axis=1, keepdims=True)
    normed = residual * lax.rsqrt(mean_square + 1e-05) * norm_gain[None, :]
    row_scale = jnp.max(jnp.abs(normed), axis=1)
    quantized = (normed / row_scale[:, None]).astype(jnp.bfloat16)
    all_rows, all_scales = (
        lax.all_gather(quantized, "tensor", axis=0, tiled=True),
        lax.all_gather(row_scale.astype(jnp.bfloat16), "tensor", axis=0, tiled=True).astype(
            row_scale.dtype
        ),
    )
    return (residual.astype(jnp.bfloat16), all_rows, all_scales)


def solution(mesh):
    return jax.shard_map(
        body,
        mesh=mesh,
        in_specs=(
            P(("dp", "tensor"), None),
            P("dp", "tensor"),
            P("dp", "tensor"),
            P("tensor", None),
            P(),
        ),
        out_specs=(P(("dp", "tensor"), None), P("dp", None), P("dp")),
        check_vma=False,
    )
```

profile of v0, /device:TPU:0, one launch (start us, length us, event | category | flops | bytes accessed | tf_op | source)
XLA Modules:
  0.0 74.4 jit_solution(3398562482728951784)
XLA Ops:
  7.2 0.0 copy-start.2
  7.2 0.0 copy-start
  7.2 0.0 copy-start.1
  7.2 0.0 reduce-scatter.2.cloned.1.call-start
  7.2 6.9 %convolution_convert_fusion = bf16[64,4096]{1,0:T(8,128)(2,1)} fusion(bf16[1280,4096]{1,0:T(8,128)(2,1)} %param.8, bf16[64,1280]{1,0:T(8,128)(2,1)} %param.7, bf16[64,1280]{1,0:T(8,128)(2,1)} %param.6), kind=kOutput, calls=%fused_computation | convolution fusion | flops 672006144 | bytes 11337728 | tf_op jit(solution)/shard_map/dot_general | solution.py:11
  14.2 0.0 reduce-scatter.2.cloned.1.call-update
  14.2 0.0 copy-done.2
  14.2 0.6 dynamic-slice
  15.4 23.2 %reduce-scatter.2.cloned.1.call-done = bf16[16,4096]{1,0:T(8,128)(2,1)} async-done(((bf16[64,4096]{1,0:T(8,128)(2,1)}), bf16[16,4096]{1,0:T(8,128)(2,1)}) %reduce-scatter.2.cloned.1.call-update) | async-done | bytes 131088 | tf_op jit(solution)/shard_map/reduce_scatter | solution.py:12
  38.7 0.0 copy-done
  38.7 1.1 %multiply_reduce_fusion = f32[16]{0:T(128)S(1)} fusion(bf16[16,4096]{1,0:T(8,128)(2,1)} %reduce-scatter.2.cloned.1.call-done, bf16[16,4096]{1,0:T(8,128)(2,1)S(1)} %copy-done), kind=kLoop, calls=%fused_computation.11 | loop fusion | flops 327664 | bytes 262208 | tf_op jit(solution)/shard_map/reduce_sum | solution.py:16
  39.8 0.0 copy-done.1
  39.8 1.1 %abs_reduce_fusion = f32[16]{0:T(128)S(1)} fusion(bf16[16,4096]{1,0:T(8,128)(2,1)} %reduce-scatter.2.cloned.1.call-done, bf16[16,4096]{1,0:T(8,128)(2,1)S(1)} %copy-done, f32[4096]{0:T(1024)S(1)} %copy-done.1, f32[16]{0:T(128)S(1)} %add_rsqrt_fusion), kind=kLoop, calls=%fused_computation.9 | loop fusion | flops 458736 | bytes 278656 | tf_op jit(solution)/shard_map/reduce_max | solution.py:18
  40.9 0.2 dynamic-update-slice
  41.1 8.7 %all-reduce = bf16[64]{0:T(256)(128)(2,1)S(1)} all-reduce(bf16[64]{0:T(256)(128)(2,1)S(1)} %dynamic-update-slice), channel_id=1, replica_groups=mesh['dp'=8,'tensor'=4] {'tensor'}, use_global_device_ids=true, to_apply=%add | all-reduce | flops 64 | bytes 256
  49.8 0.5 convert_element_type.39
  50.3 1.6 %divide_convert_fusion = (bf16[16,4096]{1,0:T(8,128)(2,1)S(1)}, bf16[16,4096]{1,0:T(8,128)(2,1)}) fusion(bf16[16,4096]{1,0:T(8,128)(2,1)} %reduce-scatter.2.cloned.1.call-done, bf16[16,4096]{1,0:T(8,128)(2,1)S(1)} %copy-done, f32[16]{0:T(128)S(1)} %abs_reduce_fusion, f32[4096]{0:T(1024)S(1)} %copy-done.1, f32[16]{0:T(128)S(1)} %add_rsqrt_fusion), kind=kLoop, calls=%fused_computation.8 | loop fusion | flops 524288 | bytes 540800 | tf_op jit(solution)/shard_map/convert_element_type | solution.py:19
  51.9 14.9 %all_gather.6 = bf16[64,4096]{1,0:T(8,128)(2,1)S(1)} all-gather(bf16[16,4096]{1,0:T(8,128)(2,1)S(1)} %get-tuple-element.3), channel_id=1, replica_groups=mesh['dp'=8,'tensor'=4] {'tensor'}, dimensions={0}, use_global_device_ids=true | all-gather | bytes 655360 | tf_op jit(solution)/shard_map/all_gather | solution.py:21
  66.8 0.8 %copy.10 = bf16[64,4096]{1,0:T(8,128)(2,1)} copy(bf16[64,4096]{1,0:T(8,128)(2,1)S(1)} %all_gather.6) | data formatting | bytes 1048576
  (3 shorter events, 0.0 us)
Async XLA Ops:
  7.2 7.0 %copy-start.2 = (u32[32]{0:T(128)S(1)}, u32[32]{0:T(128)}, u32[]{:S(2)}) copy-start(u32[32]{0:T(128)} %constant.15) | copy-start | bytes 388
  7.2 31.5 %copy-start = (bf16[16,4096]{1,0:T(8,128)(2,1)S(1)}, bf16[16,4096]{1,0:T(8,128)(2,1)}, u32[]{:S(2)}) copy-start(bf16[16,4096]{1,0:T(8,128)(2,1)} %param.5) | copy-start | bytes 393220
  7.2 32.6 %copy-start.1 = (f32[4096]{0:T(1024)S(1)}, f32[4096]{0:T(1024)}, u32[]{:S(2)}) copy-start(f32[4096]{0:T(1024)} %param.9) | copy-start | bytes 49156
  7.2 31.5 %reduce-scatter.2.cloned.1.call-start = ((), (), s32[]{:S(2)}) async-start(), calls=%async_computation.1 | async-start | bytes 655360 | tf_op jit(solution)/shard_map/reduce_scatter | solution.py:12
Sparse Core Ops, SparseCore 0:
  14.3 24.3 reduce-scatter.1
where the time goes:
time: 74.7 us; the launch traced here: 74.4 us
  blocking collectives  23.5 us (31%)
  waiting for transfers between devices  23.3 us (31%)
  between operations  14.7 us (20%)
  matrix products  6.92 us (9%)
  other arithmetic  4.29 us (6%)
  local copies, waits for them, and re-layouts  1.64 us (2%)
    reduce_scatter x1, waiting for transfers between devices, body(): lax.psum_scatter(product.astype(jnp.bfloat16), 'tensor', scatter_dimensio...  23.2 us
    all_gather x1, blocking collectives, body(): lax.all_gather(quantized, 'tensor', axis=0, tiled=True)  14.9 us
    unnamed x1, blocking collectives  8.68 us
    dot_general x1, matrix products, body(): product = jnp.dot(hidden, down_weight, preferred_element_type=jnp.float32)  6.92 us
    unnamed x10, local copies, waits for them, and re-layouts  1.64 us
    convert_element_type x1, other arithmetic, body(): quantized = (normed / row_scale[:, None]).astype(jnp.bfloat16)  1.59 us
  transfers between devices with their start and end apart: 1, of which 1 were waited for; matrix products, arithmetic and copies ran while one was open for 1% of the time, Pallas kernels for 0%

commit v1 on v0

v1 whole, which is shorter than its diff:
```python
import functools

import jax
import jax.numpy as jnp
from jax import lax
from jax.experimental import pallas as pl
from jax.experimental.pallas import tpu as pltpu
from jax.sharding import PartitionSpec as P

F32, BF16 = jnp.float32, jnp.bfloat16
SHARES = (1,1)
VMEM_LIMIT = 32 * 1024 * 1024


def spans_of(half):
    whole, at, spans = sum(SHARES), 0, []
    for share in SHARES:
        width = half * share // whole // 128 * 128
        spans.append([at, width])
        at += width
    spans[-1][1] = half - spans[-1][0]
    return [tuple(span) for span in spans]


def project_kernel(n, half, spans, keep, gated, *refs):
    k = len(spans)
    if gated:
        gate_hbm, up_hbm, tokens_hbm, weight_ref, *refs = refs
    else:
        hidden_ref, tokens_hbm, weight_ref, *refs = refs
    outs, refs = refs[:k], refs[k:]
    if gated:
        hidden_ref, gate_ref, up_ref, *refs = refs
    tokens_ref, *refs = refs
    buffers, sem = refs[:k], refs[k]
    me = lax.axis_index("tensor")
    side = lax.rem(me, 2) if keep else 1 - lax.rem(me, 2)

    def fetch(source, target, i):
        copy = pltpu.make_async_copy(source, target, sem.at[i])
        copy.start()
        return copy

    if gated:
        gating = [fetch(gate_hbm, gate_ref, k + 1), fetch(up_hbm, up_ref, k + 2)]
    copies = []
    for i, (at, width) in enumerate(spans):
        cols = pl.ds(pl.multiple_of(side * half + at, 128), width)
        copies.append(fetch(weight_ref.at[:, cols], buffers[i], i))
        if i == 0:
            adding = fetch(tokens_hbm, tokens_ref, k)
    if gated:
        for copy in gating:
            copy.wait()
        gate = gate_ref[...].astype(F32)
        hidden_ref[...] = (gate / (1.0 + jnp.exp(-gate)) * up_ref[...].astype(F32)).astype(BF16)
    rows = tokens_ref.shape[0]
    for i, (at, width) in enumerate(spans):
        copies[i].wait()
        if i == 0:
            adding.wait()
        cols = pl.ds(pl.multiple_of(side * half + at, 128), width)
        own = jnp.concatenate([tokens_ref[:, cols].astype(F32)] * n, axis=0)
        owner = lax.broadcasted_iota(jnp.int32, own.shape, 0) // rows
        product = jnp.dot(hidden_ref[...], buffers[i][...], preferred_element_type=F32)
        outs[i][...] = (product + jnp.where(owner == me, own, 0.0)).astype(BF16)


def project(n, spans, keep, gated, ins, tokens, weight):
    depth, width = weight.shape
    rows = tokens.shape[0] * n
    vmem, hbm = pl.BlockSpec(memory_space=pltpu.VMEM), pl.BlockSpec(memory_space=pltpu.HBM)
    shapes = [jax.ShapeDtypeStruct((rows, w), BF16) for _, w in spans]
    scratch = [pltpu.VMEM(tokens.shape, BF16)]
    if gated:
        shapes.append(jax.ShapeDtypeStruct((rows, depth), BF16))
        scratch = [pltpu.VMEM((rows, depth), BF16)] * 2 + scratch
    columns = sum(w for _, w in spans)
    pinned = [*(ins if gated else ()), tokens, weight]
    pinned = [pltpu.with_memory_space_constraint(x, pltpu.HBM) for x in pinned]
    return pl.pallas_call(
        functools.partial(project_kernel, n, width // 2, spans, keep, gated),
        out_shape=shapes,
        in_specs=[hbm if gated else vmem] * len(ins) + [hbm, hbm],
        out_specs=[vmem] * len(shapes),
        scratch_shapes=scratch
        + [pltpu.VMEM((depth, w), BF16) for _, w in spans]
        + [pltpu.SemaphoreType.DMA((len(spans) + 3,))],
        compiler_params=pltpu.CompilerParams(vmem_limit_bytes=VMEM_LIMIT),
        cost_estimate=pl.CostEstimate(
            flops=2 * rows * depth * columns,
            bytes_accessed=2 * depth * columns,
            transcendentals=0,
        ),
    )(*(() if gated else ins), *pinned)


def norm_kernel(half, spans, *refs):
    k = len(spans)
    own, other = refs[:k], refs[k : 2 * k]
    gain_ref, residual_ref, rows_ref, scale_ref, scaled_ref = refs[2 * k :]
    me = lax.axis_index("tensor")
    side = lax.rem(me, 2)
    mine = pl.ds(pl.multiple_of(me * residual_ref.shape[0], 16), residual_ref.shape[0])
    squares, largest = 0.0, 0.0
    for base, pieces in ((side * half, own), ((1 - side) * half, other)):
        for (at, width), piece in zip(spans, pieces):
            cols = pl.ds(pl.multiple_of(base + at, 128), width)
            residual_ref[:, cols] = piece[mine, :]
            residual = piece[...].astype(F32)
            scaled = residual * gain_ref[:, cols]
            scaled_ref[:, cols] = scaled
            squares += jnp.sum(residual * residual, axis=1, keepdims=True)
            largest = jnp.maximum(largest, jnp.max(jnp.abs(scaled), axis=1, keepdims=True))
    rows_ref[...] = (scaled_ref[...] * (1.0 / largest)).astype(BF16)
    scale_ref[...] = (largest * lax.rsqrt(squares * (0.5 / half) + 1e-05)).reshape(-1)


def norm(rows, spans, own, other, gain):
    count, width = own[0].shape[0], gain.shape[0]
    vmem = pl.BlockSpec(memory_space=pltpu.VMEM)
    return pl.pallas_call(
        functools.partial(norm_kernel, width // 2, spans),
        out_shape=[
            jax.ShapeDtypeStruct((rows, width), BF16),
            jax.ShapeDtypeStruct((count, width), BF16),
            jax.ShapeDtypeStruct((count,), F32),
        ],
        in_specs=[vmem] * (2 * len(spans) + 1),
        out_specs=[vmem] * 3,
        scratch_shapes=[pltpu.VMEM((count, width), F32)],
        compiler_params=pltpu.CompilerParams(vmem_limit_bytes=VMEM_LIMIT),
    )(*own, *other, gain.reshape(1, width))


def body(n, tokens, gate_act, up_act, down_weight, norm_gain):
    half = down_weight.shape[1] // 2
    spans = spans_of(half)
    first, hidden = project(n, spans[:1], False, True, (gate_act, up_act), tokens, down_weight)
    sent = [first, *project(n, spans[1:], False, False, (hidden,), tokens, down_weight)]
    kept = project(n, spans, True, False, (hidden,), tokens, down_weight)

    def swap(x, bit):
        return lax.ppermute(x, "tensor", [(i, i ^ bit) for i in range(n)])

    def add(a, b):
        return (a.astype(F32) + b.astype(F32)).astype(BF16)

    arrived = [swap(x, 1) for x in sent]
    sums = [add(a, b) for a, b in zip(kept, arrived)]
    bit = 2
    while bit < n:
        sums = [add(x, swap(x, bit)) for x in sums]
        bit *= 2
    others = [swap(x, 1) for x in sums]
    residual_out, next_rows, next_scale = norm(tokens.shape[0], spans, sums, others, norm_gain)
    return residual_out, next_rows, next_scale


def solution(mesh):
    n = mesh.shape["tensor"]
    return jax.shard_map(
        lambda *args: body(n, *args),
        mesh=mesh,
        in_specs=(
            P(("dp", "tensor"), None),
            P("dp", "tensor"),
            P("dp", "tensor"),
            P("tensor", None),
            P(),
        ),
        out_specs=(P(("dp", "tensor"), None), P("dp", None), P("dp")),
        check_vma=False,
    )
```

time: 74.7 us -> 33.8 us (0.45)
  blocking collectives: 23.5 us -> 0 us
  between operations: 14.7 us -> 0.68 us
  starting transfers between devices: 0.04 us -> 9.69 us
  waiting for transfers between devices: 23.3 us -> 13.9 us
  Pallas kernels: 0 us -> 9.2 us
  matrix products: 6.92 us -> 0 us
  other arithmetic: 4.29 us -> 0.14 us
  local copies, waits for them, and re-layouts: 1.64 us -> 0.01 us
    reduce_scatter x1 -> x0, waiting for transfers between devices: 23.2 us -> none  [body(): lax.psum_scatter(product.astype(jnp.bfloat16), 'tensor', scatter_dimensio...]
    all_gather x1 -> x0, blocking collectives: 14.9 us -> none  [body(): lax.all_gather(quantized, 'tensor', axis=0, tiled=True)]
    ppermute x0 -> x6, waiting for transfers between devices: none -> 13.9 us  [swap(): return lax.ppermute(x, 'tensor', [(i, i ^ bit) for i in range(n)])]
    ppermute x0 -> x6, starting transfers between devices: none -> 9.69 us  [swap(): return lax.ppermute(x, 'tensor', [(i, i ^ bit) for i in range(n)])]
    pallas_call x0 -> x4, Pallas kernels: none -> 9.2 us  [the longest x3 8.09 us: project(): pl.pallas_call(functools.partial(project_kernel, n, width // 2, spans, ke...]
    unnamed x1 -> x0, blocking collectives: 8.68 us -> none
    dot_general x1 -> x0, matrix products: 6.92 us -> none  [body(): product = jnp.dot(hidden, down_weight, preferred_element_type=jnp.float32)]
    convert_element_type x3 -> x4, other arithmetic: 2.11 us -> 0.14 us  [add(): return (a.astype(F32) + b.astype(F32)).astype(BF16)]
  transfers between devices with their start and end apart: 1 -> 6, of which waited for: 1 -> 5; matrix products, arithmetic and copies ran while one was open for 1% -> 0% of each run, Pallas kernels for 0% -> 10%
where the time goes in v1:
time: 33.8 us; the launch traced here: 33.6 us
  waiting for transfers between devices  13.9 us (41%)
  starting transfers between devices  9.69 us (29%)
  Pallas kernels  9.2 us (27%)
  between operations  0.68 us (2%)
    ppermute x6, waiting for transfers between devices, swap(): return lax.ppermute(x, 'tensor', [(i, i ^ bit) for i in range(n)])  13.9 us
    ppermute x6, starting transfers between devices, swap(): return lax.ppermute(x, 'tensor', [(i, i ^ bit) for i in range(n)])  9.69 us
    pallas_call x3, Pallas kernels, project(): pl.pallas_call(functools.partial(project_kernel, n, width // 2, spans, ke...  8.09 us
    pallas_call x1, Pallas kernels, norm(): pl.pallas_call(functools.partial(norm_kernel, width // 2, spans), out_sha...  1.11 us
  transfers between devices with their start and end apart: 6, of which 5 were waited for; matrix products, arithmetic and copies ran while one was open for 0% of the time, Pallas kernels for 10%

profile of v1, /device:TPU:0, one launch (start us, length us, event | category | flops | bytes accessed | tf_op | source)
XLA Modules:
  0.0 33.6 jit_solution(8293069773936832654)
XLA Ops:
  0.6 2.5 %shard_map.76 = (bf16[64,1024]{1,0:T(8,128)(2,1)S(1)}, bf16[64,1280]{1,0:T(8,128)(2,1)S(1)}) custom-call(bf16[64,1280]{1,0:T(8,128)(2,1)} %refs_0_.1, bf16[64,1280]{1,0:T(8,128)(2,1)} %refs_1_.3, bf16[16,4096]{1,0:T(8,128)(2,1)} %refs_1_.5, bf16[1280,4096]{1,0:T(8,128)(2,1)} %refs_2_.5), custom_call_target="tpu_custom_call" | custom-call | flops 167772160 | bytes 2621440 | tf_op jit(solution)/shard_map/pallas_call | solution.py:81
  3.2 0.0 copy-start
  3.2 2.4 %shard_map.78 = bf16[64,1024]{1,0:T(8,128)(2,1)S(1)} custom-call(bf16[64,1280]{1,0:T(8,128)(2,1)S(1)} %get-tuple-element.7.refs_0_, bf16[16,4096]{1,0:T(8,128)(2,1)} %refs_1_.5, bf16[1280,4096]{1,0:T(8,128)(2,1)} %refs_2_.5), custom_call_target="tpu_custom_call" | custom-call | flops 167772160 | bytes 2621440 | tf_op jit(solution)/shard_map/pallas_call | solution.py:81
  5.6 3.1 %collective-permute-start.2 = (bf16[64,1024]{1,0:T(8,128)(2,1)S(1)}, bf16[64,1024]{1,0:T(8,128)(2,1)S(1)}, u32[]{:S(2)}, u32[]{:S(2)}) collective-permute-start(bf16[64,1024]{1,0:T(8,128)(2,1)S(1)} %shard_map.78), channel_id=1, source_target_pairs={{0,1},{1,0},{2,3},{3,2},{4,5},{5,4},{6,7},{7,6},{8,9},{9,8},{10,11... | collective-permute-start | bytes 393224 | tf_op jit(solution)/shard_map/ppermute | solution.py:144
  8.6 0.1 collective-permute-start
  8.7 3.2 %shard_map.77 = (bf16[64,1024]{1,0:T(8,128)(2,1)S(1)}, bf16[64,1024]{1,0:T(8,128)(2,1)S(1)}) custom-call(bf16[64,1280]{1,0:T(8,128)(2,1)S(1)} %get-tuple-element.7.refs_0_, bf16[16,4096]{1,0:T(8,128)(2,1)} %refs_1_.5, bf16[1280,4096]{1,0:T(8,128)(2,1)} %refs_2_.5), custom_call_target="tpu_custom_call" | custom-call | flops 335544320 | bytes 5242880 | tf_op jit(solution)/shard_map/pallas_call | solution.py:81
  11.9 1.0 %collective-permute-done.2 = bf16[64,1024]{1,0:T(8,128)(2,1)S(1)} collective-permute-done((bf16[64,1024]{1,0:T(8,128)(2,1)S(1)}, bf16[64,1024]{1,0:T(8,128)(2,1)S(1)}, u32[]{:S(2)}, u32[]{:S(2)}) %collective-permute-start.2) | collective-permute-done | bytes 131104 | tf_op jit(solution)/shard_map/ppermute | solution.py:144
  13.0 3.1 %collective-permute-start.3 = (bf16[64,1024]{1,0:T(8,128)(2,1)S(1)}, bf16[64,1024]{1,0:T(8,128)(2,1)S(1)}, u32[]{:S(2)}, u32[]{:S(2)}) collective-permute-start(bf16[64,1024]{1,0:T(8,128)(2,1)S(1)} %add_convert_fusion.1), channel_id=1, source_target_pairs={{0,2},{1,3},{2,0},{3,1},{4,6},{5,7},{6,4},{7,5},{8,10},{9,11},{10,... | collective-permute-start | bytes 393224 | tf_op jit(solution)/shard_map/ppermute | solution.py:144
  16.1 0.0 collective-permute-done
  16.2 2.5 %collective-permute-start.1 = (bf16[64,1024]{1,0:T(8,128)(2,1)S(1)}, bf16[64,1024]{1,0:T(8,128)(2,1)S(1)}, u32[]{:S(2)}, u32[]{:S(2)}) collective-permute-start(bf16[64,1024]{1,0:T(8,128)(2,1)S(1)} %add_convert_fusion.3), channel_id=1, source_target_pairs={{0,2},{1,3},{2,0},{3,1},{4,6},{5,7},{6,4},{7,5},{8,10},{9,11},{10,... | collective-permute-start | bytes 393224 | tf_op jit(solution)/shard_map/ppermute | solution.py:144
  18.7 6.7 %collective-permute-done.3 = bf16[64,1024]{1,0:T(8,128)(2,1)S(1)} collective-permute-done((bf16[64,1024]{1,0:T(8,128)(2,1)S(1)}, bf16[64,1024]{1,0:T(8,128)(2,1)S(1)}, u32[]{:S(2)}, u32[]{:S(2)}) %collective-permute-start.3) | collective-permute-done | bytes 131104 | tf_op jit(solution)/shard_map/ppermute | solution.py:144
  25.5 0.2 collective-permute-start.5
  25.6 1.3 %collective-permute-done.1 = bf16[64,1024]{1,0:T(8,128)(2,1)S(1)} collective-permute-done((bf16[64,1024]{1,0:T(8,128)(2,1)S(1)}, bf16[64,1024]{1,0:T(8,128)(2,1)S(1)}, u32[]{:S(2)}, u32[]{:S(2)}) %collective-permute-start.1) | collective-permute-done | bytes 131104 | tf_op jit(solution)/shard_map/ppermute | solution.py:144
  27.0 0.7 %collective-permute-start.4 = (bf16[64,1024]{1,0:T(8,128)(2,1)S(1)}, bf16[64,1024]{1,0:T(8,128)(2,1)S(1)}, u32[]{:S(2)}, u32[]{:S(2)}) collective-permute-start(bf16[64,1024]{1,0:T(8,128)(2,1)S(1)} %add_convert_fusion.2.refs_0_), channel_id=1, source_target_pairs={{0,1},{1,0},{2,3},{3,2},{4,5},{5,4},{6,7},{7,6},{8,9},{9,8},{10,11... | collective-permute-start | bytes 393224 | tf_op jit(solution)/shard_map/ppermute | solution.py:144
  27.7 3.4 %collective-permute-done.5.refs_3_ = bf16[64,1024]{1,0:T(8,128)(2,1)S(1)} collective-permute-done((bf16[64,1024]{1,0:T(8,128)(2,1)S(1)}, bf16[64,1024]{1,0:T(8,128)(2,1)S(1)}, u32[]{:S(2)}, u32[]{:S(2)}) %collective-permute-start.5) | collective-permute-done | bytes 131104 | tf_op jit(solution)/shard_map/ppermute | solution.py:144
  31.1 1.4 %collective-permute-done.4.refs_2_ = bf16[64,1024]{1,0:T(8,128)(2,1)S(1)} collective-permute-done((bf16[64,1024]{1,0:T(8,128)(2,1)S(1)}, bf16[64,1024]{1,0:T(8,128)(2,1)S(1)}, u32[]{:S(2)}, u32[]{:S(2)}) %collective-permute-start.4) | collective-permute-done | bytes 131104 | tf_op jit(solution)/shard_map/ppermute | solution.py:144
  32.5 0.0 copy-done
  32.5 1.1 %shard_map.79 = (bf16[16,4096]{1,0:T(8,128)(2,1)}, bf16[64,4096]{1,0:T(8,128)(2,1)}, f32[64]{0:T(128)}) custom-call(bf16[64,1024]{1,0:T(8,128)(2,1)S(1)} %add_convert_fusion.2.refs_0_, bf16[64,1024]{1,0:T(8,128)(2,1)S(1)} %add_convert_fusion.refs_1_, bf16[64,1024]{1,0:T(8,128)(2,1)S(1)} %collective-permute-done.4.refs_2_, ...), custom_call_target="tpu_custom_call" | custom-call | tf_op jit(solution)/shard_map/pallas_call | solution.py:122
  (4 shorter events, 0.1 us)
Async XLA Ops:
  3.2 29.3 %copy-start = (f32[4096]{0:T(1024)S(1)}, f32[4096]{0:T(1024)}, u32[]{:S(2)}) copy-start(f32[4096]{0:T(1024)} %param.9) | copy-start | bytes 49156
  5.6 7.4 %collective-permute-start.2 = (bf16[64,1024]{1,0:T(8,128)(2,1)S(1)}, bf16[64,1024]{1,0:T(8,128)(2,1)S(1)}, u32[]{:S(2)}, u32[]{:S(2)}) collective-permute-start(bf16[64,1024]{1,0:T(8,128)(2,1)S(1)} %shard_map.78), channel_id=1, source_target_pairs={{0,1},{1,0},{2,3},{3,2},{4,5},{5,4},{6,7},{7,6},{8,9},{9,8},{10,11... | collective-permute-start | bytes 393224 | tf_op jit(solution)/shard_map/ppermute | solution.py:144
  8.6 7.5 %collective-permute-start = (bf16[64,1024]{1,0:T(8,128)(2,1)S(1)}, bf16[64,1024]{1,0:T(8,128)(2,1)S(1)}, u32[]{:S(2)}, u32[]{:S(2)}) collective-permute-start(bf16[64,1024]{1,0:T(8,128)(2,1)S(1)} %get-tuple-element.9), channel_id=1, source_target_pairs={{0,1},{1,0},{2,3},{3,2},{4,5},{5,4},{6,7},{7,6},{8,9},{9,8},{10,11... | collective-permute-start | bytes 393224 | tf_op jit(solution)/shard_map/ppermute | solution.py:144
  13.0 12.4 %collective-permute-start.3 = (bf16[64,1024]{1,0:T(8,128)(2,1)S(1)}, bf16[64,1024]{1,0:T(8,128)(2,1)S(1)}, u32[]{:S(2)}, u32[]{:S(2)}) collective-permute-start(bf16[64,1024]{1,0:T(8,128)(2,1)S(1)} %add_convert_fusion.1), channel_id=1, source_target_pairs={{0,2},{1,3},{2,0},{3,1},{4,6},{5,7},{6,4},{7,5},{8,10},{9,11},{10,... | collective-permute-start | bytes 393224 | tf_op jit(solution)/shard_map/ppermute | solution.py:144
  16.2 10.7 %collective-permute-start.1 = (bf16[64,1024]{1,0:T(8,128)(2,1)S(1)}, bf16[64,1024]{1,0:T(8,128)(2,1)S(1)}, u32[]{:S(2)}, u32[]{:S(2)}) collective-permute-start(bf16[64,1024]{1,0:T(8,128)(2,1)S(1)} %add_convert_fusion.3), channel_id=1, source_target_pairs={{0,2},{1,3},{2,0},{3,1},{4,6},{5,7},{6,4},{7,5},{8,10},{9,11},{10,... | collective-permute-start | bytes 393224 | tf_op jit(solution)/shard_map/ppermute | solution.py:144
  25.5 5.6 %collective-permute-start.5 = (bf16[64,1024]{1,0:T(8,128)(2,1)S(1)}, bf16[64,1024]{1,0:T(8,128)(2,1)S(1)}, u32[]{:S(2)}, u32[]{:S(2)}) collective-permute-start(bf16[64,1024]{1,0:T(8,128)(2,1)S(1)} %add_convert_fusion.refs_1_), channel_id=1, source_target_pairs={{0,1},{1,0},{2,3},{3,2},{4,5},{5,4},{6,7},{7,6},{8,9},{9,8},{10,11... | collective-permute-start | bytes 393224 | tf_op jit(solution)/shard_map/ppermute | solution.py:144
  27.0 5.5 %collective-permute-start.4 = (bf16[64,1024]{1,0:T(8,128)(2,1)S(1)}, bf16[64,1024]{1,0:T(8,128)(2,1)S(1)}, u32[]{:S(2)}, u32[]{:S(2)}) collective-permute-start(bf16[64,1024]{1,0:T(8,128)(2,1)S(1)} %add_convert_fusion.2.refs_0_), channel_id=1, source_target_pairs={{0,1},{1,0},{2,3},{3,2},{4,5},{5,4},{6,7},{7,6},{8,9},{9,8},{10,11... | collective-permute-start | bytes 393224 | tf_op jit(solution)/shard_map/ppermute | solution.py:144

commit v2 on v1

v2 whole, which is shorter than its diff:
```python
import functools

import jax
import jax.numpy as jnp
from jax import lax
from jax.experimental import pallas as pl
from jax.experimental.pallas import tpu as pltpu
from jax.sharding import PartitionSpec as P

F32, BF16 = jnp.float32, jnp.bfloat16
TILE = 512
CHUNKS = ((7, 2, True), (9, 1, True))
PLAN = (((0, False), (1, False)), ((0, True), (1, True)))
AFTER = {}
VMEM_LIMIT = 32 * 1024 * 1024


def chunks_of(n, width):
    whole, at, chunks = sum(share for share, _, _ in CHUNKS), 0, []
    for share, first, halved in CHUNKS:
        first = min(first, n // 2)
        bits = [1 << i for i in range(n.bit_length() - 1)]
        bits = [first, *(bit for bit in bits if bit != first)]
        wide = width * share // whole // 256 * 256
        if len(chunks) == len(CHUNKS) - 1:
            wide = width - at
        chunks.append((bits, halved, at, wide // 2 if halved else wide))
        at += wide
    return chunks


def side_of(me, bit):
    return lax.rem(lax.div(me, bit), 2)


def tiles_of(blocks):
    tiles = []
    for i, (*_, width, _) in enumerate(blocks):
        count = -(-width // TILE)
        piece = -(-width // count // 128) * 128
        tiles += [(i, c, min(piece, width - c)) for c in range(0, width, piece)]
    return tiles


def project_kernel(n, blocks, gated, waited, *refs):
    k = len(blocks)
    refs = refs[waited:]
    tiles = tiles_of(blocks)
    if gated:
        gate_hbm, up_hbm, tokens_hbm, weight_ref, *refs = refs
    else:
        hidden_ref, tokens_hbm, weight_ref, *refs = refs
    outs, refs = refs[:k], refs[k:]
    if gated:
        hidden_ref, gate_ref, up_ref, *refs = refs
    tokens_ref, *buffers, sem = refs
    me = lax.axis_index("tensor")

    def fetch(source, target, i):
        copy = pltpu.make_async_copy(source, target, sem.at[i])
        copy.start()
        return copy

    def columns(i, c, width):
        bits, halved, at, block, keep = blocks[i]
        if halved:
            side = side_of(me, bits[0])
            at += (side if keep else 1 - side) * block
        return pl.ds(pl.multiple_of(at + c, 128), width)

    if gated:
        gating = [fetch(gate_hbm, gate_ref, 1), fetch(up_hbm, up_ref, 2)]
    copies = []
    for j, tile in enumerate(tiles):
        copies.append(fetch(weight_ref.at[:, columns(*tile)], buffers[j], 3 + j))
        if j == 0:
            adding = fetch(tokens_hbm, tokens_ref, 0)
    if gated:
        for copy in gating:
            copy.wait()
        gate = gate_ref[...].astype(F32)
        hidden_ref[...] = (gate / (1.0 + jnp.exp(-gate)) * up_ref[...].astype(F32)).astype(BF16)
    rows = tokens_ref.shape[0]
    adding.wait()
    for j, tile in enumerate(tiles):
        i, c, width = tile
        own = jnp.concatenate([tokens_ref[:, columns(*tile)].astype(F32)] * n, axis=0)
        owner = lax.broadcasted_iota(jnp.int32, own.shape, 0) // rows
        copies[j].wait()
        product = jnp.dot(hidden_ref[...], buffers[j][...], preferred_element_type=F32)
        outs[i][:, c : c + width] = (product + jnp.where(owner == me, own, 0.0)).astype(BF16)


def project(n, blocks, gated, ins, tokens, weight, after=()):
    depth = weight.shape[0]
    rows = tokens.shape[0] * n
    vmem, hbm = pl.BlockSpec(memory_space=pltpu.VMEM), pl.BlockSpec(memory_space=pl.ANY)
    shapes = [jax.ShapeDtypeStruct((rows, w), BF16) for *_, w, _ in blocks]
    scratch = [pltpu.VMEM(tokens.shape, BF16)]
    if gated:
        shapes.append(jax.ShapeDtypeStruct((rows, depth), BF16))
        scratch = [pltpu.VMEM((rows, depth), BF16)] * 2 + scratch
    columns = sum(w for *_, w, _ in blocks)
    tiles = tiles_of(blocks)
    pinned = [*(ins if gated else ()), tokens, weight]
    pinned = [pltpu.with_memory_space_constraint(x, pltpu.HBM) for x in pinned]
    return pl.pallas_call(
        functools.partial(project_kernel, n, blocks, gated, len(after)),
        out_shape=shapes,
        in_specs=[hbm] * len(after) + [hbm if gated else vmem] * len(ins) + [hbm, hbm],
        out_specs=[vmem] * len(shapes),
        scratch_shapes=scratch
        + [pltpu.VMEM((depth, w), BF16) for _, _, w in tiles]
        + [pltpu.SemaphoreType.DMA((len(tiles) + 3,))],
        compiler_params=pltpu.CompilerParams(vmem_limit_bytes=VMEM_LIMIT),
        cost_estimate=pl.CostEstimate(
            flops=2 * rows * depth * columns,
            bytes_accessed=2 * depth * columns,
            transcendentals=0,
        ),
    )(*after, *(() if gated else ins), *pinned)


def norm_kernel(chunks, *refs):
    *pieces, gain_ref, residual_ref, rows_ref, scale_ref, scaled_ref = refs
    me = lax.axis_index("tensor")
    mine = pl.ds(pl.multiple_of(me * residual_ref.shape[0], 16), residual_ref.shape[0])
    squares, largest = 0.0, 0.0
    pieces = iter(pieces)
    for bits, halved, at, width in chunks:
        side = side_of(me, bits[0])
        for first in (at + side * width, at + (1 - side) * width) if halved else (at,):
            piece = next(pieces)
            cols = pl.ds(pl.multiple_of(first, 128), width)
            residual_ref[:, cols] = piece[mine, :]
            residual = piece[...].astype(F32)
            scaled = residual * gain_ref[:, cols]
            scaled_ref[:, cols] = scaled
            squares += jnp.sum(residual * residual, axis=1, keepdims=True)
            largest = jnp.maximum(largest, jnp.max(jnp.abs(scaled), axis=1, keepdims=True))
    rows_ref[...] = (scaled_ref[...] * (1.0 / largest)).astype(BF16)
    mean = squares * (1.0 / rows_ref.shape[1])
    scale_ref[...] = (largest * lax.rsqrt(mean + 1e-05)).reshape(-1)


def norm(rows, chunks, pieces, gain):
    count, width = pieces[0].shape[0], gain.shape[0]
    vmem = pl.BlockSpec(memory_space=pltpu.VMEM)
    return pl.pallas_call(
        functools.partial(norm_kernel, chunks),
        out_shape=[
            jax.ShapeDtypeStruct((rows, width), BF16),
            jax.ShapeDtypeStruct((count, width), BF16),
            jax.ShapeDtypeStruct((count,), F32),
        ],
        in_specs=[vmem] * (len(pieces) + 1),
        out_specs=[vmem] * 3,
        scratch_shapes=[pltpu.VMEM((count, width), F32)],
        compiler_params=pltpu.CompilerParams(vmem_limit_bytes=VMEM_LIMIT),
    )(*pieces, gain.reshape(1, width))


def body(n, tokens, gate_act, up_act, down_weight, norm_gain):
    chunks = chunks_of(n, down_weight.shape[1])
    def swap(x, bit):
        return lax.ppermute(x, "tensor", [(i, i ^ bit) for i in range(n)])

    def add(a, b):
        return (a.astype(F32) + b.astype(F32)).astype(BF16)

    made, arrived = {}, {}
    for step, chosen in enumerate(PLAN):
        ins = (hidden,) if step else (gate_act, up_act)
        blocks = [(*chunks[i], keep) for i, keep in chosen]
        after = [arrived[AFTER[step]]] if step in AFTER else []
        outs = project(n, blocks, not step, ins, tokens, down_weight, after)
        if not step:
            *outs, hidden = outs
        made.update(zip(chosen, outs))
        for i, keep in chosen:
            bits, halved, _, _ = chunks[i]
            if not keep or not halved:
                arrived[i] = swap(made[i, keep], bits[0])

    pieces = []
    for i, (bits, halved, _, _) in enumerate(chunks):
        total = add(made[i, True], arrived[i])
        for bit in bits[1:]:
            total = add(total, swap(total, bit))
        pieces.append(total)
        if halved:
            pieces.append(swap(total, bits[0]))
    return norm(tokens.shape[0], chunks, pieces, norm_gain)


def solution(mesh):
    n = mesh.shape["tensor"]
    return jax.shard_map(
        lambda *args: body(n, *args),
        mesh=mesh,
        in_specs=(
            P(("dp", "tensor"), None),
            P("dp", "tensor"),
            P("dp", "tensor"),
            P("tensor", None),
            P(),
        ),
        out_specs=(P(("dp", "tensor"), None), P("dp", None), P("dp")),
        check_vma=False,
    )
```

time: 33.8 us -> 29.6 us (0.88)
  waiting for transfers between devices: 13.9 us -> 8.62 us
  starting transfers between devices: 9.69 us -> 12.6 us
  Pallas kernels: 9.2 us -> 7.32 us
    ppermute x6, waiting for transfers between devices: 13.9 us -> 8.62 us  [swap(): return lax.ppermute(x, 'tensor', [(i, i ^ bit) for i in range(n)])]
    ppermute x6, starting transfers between devices: 9.69 us -> 12.6 us  [swap(): return lax.ppermute(x, 'tensor', [(i, i ^ bit) for i in range(n)])]
    pallas_call x4 -> x3, Pallas kernels: 9.2 us -> 7.32 us  [the longest x2 6.2 us: project(): pl.pallas_call(functools.partial(project_kernel, n, blocks, gated, len(af...]
  transfers between devices with their start and end apart: 6 -> 6, of which waited for: 5 -> 4; matrix products, arithmetic and copies ran while one was open for 0% -> 0% of each run, Pallas kernels for 10% -> 10%
where the time goes in v2:
time: 29.6 us; the launch traced here: 29.4 us
  starting transfers between devices  12.6 us (43%)
  waiting for transfers between devices  8.62 us (29%)
  Pallas kernels  7.32 us (25%)
  between operations  0.7 us (2%)
    ppermute x6, starting transfers between devices, swap(): return lax.ppermute(x, 'tensor', [(i, i ^ bit) for i in range(n)])  12.6 us
    ppermute x6, waiting for transfers between devices, swap(): return lax.ppermute(x, 'tensor', [(i, i ^ bit) for i in range(n)])  8.62 us
    pallas_call x2, Pallas kernels, project(): pl.pallas_call(functools.partial(project_kernel, n, blocks, gated, len(af...  6.2 us
    pallas_call x1, Pallas kernels, norm(): pl.pallas_call(functools.partial(norm_kernel, chunks), out_shape=[jax.Sha...  1.12 us
  transfers between devices with their start and end apart: 6, of which 4 were waited for; matrix products, arithmetic and copies ran while one was open for 0% of the time, Pallas kernels for 10%

profile of v2, /device:TPU:0, one launch (start us, length us, event | category | flops | bytes accessed | tf_op | source)
XLA Modules:
  0.0 29.4 jit_solution(7913547167130704999)
XLA Ops:
  0.6 0.0 copy-start
  0.6 3.2 %shard_map.76 = (bf16[64,896]{1,0:T(8,128)(2,1)S(1)}, bf16[64,1152]{1,0:T(8,128)(2,1)S(1)}, bf16[64,1280]{1,0:T(8,128)(2,1)S(1)}) custom-call(bf16[64,1280]{1,0:T(8,128)(2,1)} %refs_0_.1, bf16[64,1280]{1,0:T(8,128)(2,1)} %refs_1_.2, bf16[16,4096]{1,0:T(8,128)(2,1)} %refs_1_.3, bf16[1280,4096]{1,0:T(8,128)(2,1)} %refs_2_.3), custom_call_target="tpu_custom_call" | custom-call | flops 335544320 | bytes 5242880 | tf_op jit(solution)/shard_map/pallas_call | solution.py:107
  3.8 3.1 %collective-permute-start.3 = (bf16[64,1152]{1,0:T(8,128)(2,1)S(1)}, bf16[64,1152]{1,0:T(8,128)(2,1)S(1)}, u32[]{:S(2)}, u32[]{:S(2)}) collective-permute-start(bf16[64,1152]{1,0:T(8,128)(2,1)S(1)} %get-tuple-element.12), channel_id=1, source_target_pairs={{0,1},{1,0},{2,3},{3,2},{4,5},{5,4},{6,7},{7,6},{8,9},{9,8},{10,11... | collective-permute-start | bytes 442376 | tf_op jit(solution)/shard_map/ppermute | solution.py:166
  6.9 2.6 %collective-permute-start = (bf16[64,896]{1,0:T(8,128)(2,1)S(1)}, bf16[64,896]{1,0:T(8,128)(2,1)S(1)}, u32[]{:S(2)}, u32[]{:S(2)}) collective-permute-start(bf16[64,896]{1,0:T(8,128)(2,1)S(1)} %get-tuple-element.10), channel_id=1, source_target_pairs={{0,2},{1,3},{2,0},{3,1},{4,6},{5,7},{6,4},{7,5},{8,10},{9,11},{10,... | collective-permute-start | bytes 344072 | tf_op jit(solution)/shard_map/ppermute | solution.py:166
  9.5 3.0 %shard_map.77 = (bf16[64,896]{1,0:T(8,128)(2,1)S(1)}, bf16[64,1152]{1,0:T(8,128)(2,1)S(1)}) custom-call(bf16[64,1280]{1,0:T(8,128)(2,1)S(1)} %get-tuple-element.8.refs_0_, bf16[16,4096]{1,0:T(8,128)(2,1)} %refs_1_.3, bf16[1280,4096]{1,0:T(8,128)(2,1)} %refs_2_.3), custom_call_target="tpu_custom_call" | custom-call | flops 335544320 | bytes 5242880 | tf_op jit(solution)/shard_map/pallas_call | solution.py:107
  12.5 0.5 %collective-permute-done.3 = bf16[64,1152]{1,0:T(8,128)(2,1)S(1)} collective-permute-done((bf16[64,1152]{1,0:T(8,128)(2,1)S(1)}, bf16[64,1152]{1,0:T(8,128)(2,1)S(1)}, u32[]{:S(2)}, u32[]{:S(2)}) %collective-permute-start.3) | collective-permute-done | bytes 147488 | tf_op jit(solution)/shard_map/ppermute | solution.py:166
  13.1 1.7 %collective-permute-start.4 = (bf16[64,1152]{1,0:T(8,128)(2,1)S(1)}, bf16[64,1152]{1,0:T(8,128)(2,1)S(1)}, u32[]{:S(2)}, u32[]{:S(2)}) collective-permute-start(bf16[64,1152]{1,0:T(8,128)(2,1)S(1)} %add_convert_fusion.1), channel_id=1, source_target_pairs={{0,2},{1,3},{2,0},{3,1},{4,6},{5,7},{6,4},{7,5},{8,10},{9,11},{10,... | collective-permute-start | bytes 442376 | tf_op jit(solution)/shard_map/ppermute | solution.py:166
  14.8 0.0 collective-permute-done
  14.8 2.4 %collective-permute-start.1 = (bf16[64,896]{1,0:T(8,128)(2,1)S(1)}, bf16[64,896]{1,0:T(8,128)(2,1)S(1)}, u32[]{:S(2)}, u32[]{:S(2)}) collective-permute-start(bf16[64,896]{1,0:T(8,128)(2,1)S(1)} %add_convert_fusion.3), channel_id=1, source_target_pairs={{0,1},{1,0},{2,3},{3,2},{4,5},{5,4},{6,7},{7,6},{8,9},{9,8},{10,11... | collective-permute-start | bytes 344072 | tf_op jit(solution)/shard_map/ppermute | solution.py:166
  17.2 4.5 %collective-permute-done.4 = bf16[64,1152]{1,0:T(8,128)(2,1)S(1)} collective-permute-done((bf16[64,1152]{1,0:T(8,128)(2,1)S(1)}, bf16[64,1152]{1,0:T(8,128)(2,1)S(1)}, u32[]{:S(2)}, u32[]{:S(2)}) %collective-permute-start.4) | collective-permute-done | bytes 147488 | tf_op jit(solution)/shard_map/ppermute | solution.py:166
  21.8 0.1 collective-permute-start.5
  21.9 0.0 collective-permute-done.1
  21.9 2.8 %collective-permute-start.2 = (bf16[64,896]{1,0:T(8,128)(2,1)S(1)}, bf16[64,896]{1,0:T(8,128)(2,1)S(1)}, u32[]{:S(2)}, u32[]{:S(2)}) collective-permute-start(bf16[64,896]{1,0:T(8,128)(2,1)S(1)} %add_convert_fusion.2.refs_0_), channel_id=1, source_target_pairs={{0,2},{1,3},{2,0},{3,1},{4,6},{5,7},{6,4},{7,5},{8,10},{9,11},{10,... | collective-permute-start | bytes 344072 | tf_op jit(solution)/shard_map/ppermute | solution.py:166
  24.7 3.2 %collective-permute-done.2.refs_1_ = bf16[64,896]{1,0:T(8,128)(2,1)S(1)} collective-permute-done((bf16[64,896]{1,0:T(8,128)(2,1)S(1)}, bf16[64,896]{1,0:T(8,128)(2,1)S(1)}, u32[]{:S(2)}, u32[]{:S(2)}) %collective-permute-start.2) | collective-permute-done | bytes 114720 | tf_op jit(solution)/shard_map/ppermute | solution.py:166
  27.9 0.4 %collective-permute-done.5.refs_3_ = bf16[64,1152]{1,0:T(8,128)(2,1)S(1)} collective-permute-done((bf16[64,1152]{1,0:T(8,128)(2,1)S(1)}, bf16[64,1152]{1,0:T(8,128)(2,1)S(1)}, u32[]{:S(2)}, u32[]{:S(2)}) %collective-permute-start.5) | collective-permute-done | bytes 147488 | tf_op jit(solution)/shard_map/ppermute | solution.py:166
  28.3 0.0 copy-done
  28.3 1.1 %shard_map.78 = (bf16[16,4096]{1,0:T(8,128)(2,1)}, bf16[64,4096]{1,0:T(8,128)(2,1)}, f32[64]{0:T(128)}) custom-call(bf16[64,896]{1,0:T(8,128)(2,1)S(1)} %add_convert_fusion.2.refs_0_, bf16[64,896]{1,0:T(8,128)(2,1)S(1)} %collective-permute-done.2.refs_1_, bf16[64,1152]{1,0:T(8,128)(2,1)S(1)} %add_convert_fusion.refs_2_, ...), custom_call_target="tpu_custom_call" | custom-call | tf_op jit(solution)/shard_map/pallas_call | solution.py:149
  (4 shorter events, 0.1 us)
Async XLA Ops:
  0.6 27.7 %copy-start = (f32[4096]{0:T(1024)S(1)}, f32[4096]{0:T(1024)}, u32[]{:S(2)}) copy-start(f32[4096]{0:T(1024)} %param.9) | copy-start | bytes 49156
  3.8 9.2 %collective-permute-start.3 = (bf16[64,1152]{1,0:T(8,128)(2,1)S(1)}, bf16[64,1152]{1,0:T(8,128)(2,1)S(1)}, u32[]{:S(2)}, u32[]{:S(2)}) collective-permute-start(bf16[64,1152]{1,0:T(8,128)(2,1)S(1)} %get-tuple-element.12), channel_id=1, source_target_pairs={{0,1},{1,0},{2,3},{3,2},{4,5},{5,4},{6,7},{7,6},{8,9},{9,8},{10,11... | collective-permute-start | bytes 442376 | tf_op jit(solution)/shard_map/ppermute | solution.py:166
  6.9 7.9 %collective-permute-start = (bf16[64,896]{1,0:T(8,128)(2,1)S(1)}, bf16[64,896]{1,0:T(8,128)(2,1)S(1)}, u32[]{:S(2)}, u32[]{:S(2)}) collective-permute-start(bf16[64,896]{1,0:T(8,128)(2,1)S(1)} %get-tuple-element.10), channel_id=1, source_target_pairs={{0,2},{1,3},{2,0},{3,1},{4,6},{5,7},{6,4},{7,5},{8,10},{9,11},{10,... | collective-permute-start | bytes 344072 | tf_op jit(solution)/shard_map/ppermute | solution.py:166
  13.1 8.7 %collective-permute-start.4 = (bf16[64,1152]{1,0:T(8,128)(2,1)S(1)}, bf16[64,1152]{1,0:T(8,128)(2,1)S(1)}, u32[]{:S(2)}, u32[]{:S(2)}) collective-permute-start(bf16[64,1152]{1,0:T(8,128)(2,1)S(1)} %add_convert_fusion.1), channel_id=1, source_target_pairs={{0,2},{1,3},{2,0},{3,1},{4,6},{5,7},{6,4},{7,5},{8,10},{9,11},{10,... | collective-permute-start | bytes 442376 | tf_op jit(solution)/shard_map/ppermute | solution.py:166
  14.8 7.0 %collective-permute-start.1 = (bf16[64,896]{1,0:T(8,128)(2,1)S(1)}, bf16[64,896]{1,0:T(8,128)(2,1)S(1)}, u32[]{:S(2)}, u32[]{:S(2)}) collective-permute-start(bf16[64,896]{1,0:T(8,128)(2,1)S(1)} %add_convert_fusion.3), channel_id=1, source_target_pairs={{0,1},{1,0},{2,3},{3,2},{4,5},{5,4},{6,7},{7,6},{8,9},{9,8},{10,11... | collective-permute-start | bytes 344072 | tf_op jit(solution)/shard_map/ppermute | solution.py:166
  21.8 6.5 %collective-permute-start.5 = (bf16[64,1152]{1,0:T(8,128)(2,1)S(1)}, bf16[64,1152]{1,0:T(8,128)(2,1)S(1)}, u32[]{:S(2)}, u32[]{:S(2)}) collective-permute-start(bf16[64,1152]{1,0:T(8,128)(2,1)S(1)} %add_convert_fusion.refs_2_), channel_id=1, source_target_pairs={{0,1},{1,0},{2,3},{3,2},{4,5},{5,4},{6,7},{7,6},{8,9},{9,8},{10,11... | collective-permute-start | bytes 442376 | tf_op jit(solution)/shard_map/ppermute | solution.py:166
  21.9 6.0 %collective-permute-start.2 = (bf16[64,896]{1,0:T(8,128)(2,1)S(1)}, bf16[64,896]{1,0:T(8,128)(2,1)S(1)}, u32[]{:S(2)}, u32[]{:S(2)}) collective-permute-start(bf16[64,896]{1,0:T(8,128)(2,1)S(1)} %add_convert_fusion.2.refs_0_), channel_id=1, source_target_pairs={{0,2},{1,3},{2,0},{3,1},{4,6},{5,7},{6,4},{7,5},{8,10},{9,11},{10,... | collective-permute-start | bytes 344072 | tf_op jit(solution)/shard_map/ppermute | solution.py:166

commit v3 on v2

--- a/solution.py
+++ b/solution.py
@@ -9,42 +9,49 @@
 
 F32, BF16 = jnp.float32, jnp.bfloat16
 TILE = 512
-CHUNKS = ((7, 2, True), (9, 1, True))
+CHUNKS = ((8, ((2, 1), (1, 2))), (8, ((1, 2), (1, 3))))
 PLAN = (((0, False), (1, False)), ((0, True), (1, True)))
-AFTER = {}
 VMEM_LIMIT = 32 * 1024 * 1024
 
 
 def chunks_of(n, width):
-    whole, at, chunks = sum(share for share, _, _ in CHUNKS), 0, []
-    for share, first, halved in CHUNKS:
-        first = min(first, n // 2)
-        bits = [1 << i for i in range(n.bit_length() - 1)]
-        bits = [first, *(bit for bit in bits if bit != first)]
+    whole, at, chunks = sum(share for share, _ in CHUNKS), 0, []
+    for share, firsts in CHUNKS:
+        rest = [1 << i for i in range(2, n.bit_length() - 1)]
+        masks = [[*first, *rest] if n > 2 else [1] for first in firsts]
         wide = width * share // whole // 256 * 256
         if len(chunks) == len(CHUNKS) - 1:
             wide = width - at
-        chunks.append((bits, halved, at, wide // 2 if halved else wide))
+        chunks.append((masks, at, wide // 2))
         at += wide
     return chunks
 
 
-def side_of(me, bit):
-    return lax.rem(lax.div(me, bit), 2)
+def parity(number):
+    return number.bit_count() % 2
+
+
+def side_of(n, masks):
+    me, core = lax.axis_index("tensor"), lax.rem(lax.axis_index("dp"), 2)
+    sides = []
+    for first, *later in masks:
+        marks = [m for m in range(n) if parity(m & first) and not any(parity(m & x) for x in later)]
+        bits = [lax.rem(lax.div(me, 1 << i), 2) for i in range(n.bit_length()) if marks[0] >> i & 1]
+        sides.append(lax.rem(sum(bits), 2))
+    return jnp.where(core == 0, sides[0], sides[1])
 
 
 def tiles_of(blocks):
     tiles = []
-    for i, (*_, width, _) in enumerate(blocks):
+    for i, (_, _, width, _) in enumerate(blocks):
         count = -(-width // TILE)
         piece = -(-width // count // 128) * 128
         tiles += [(i, c, min(piece, width - c)) for c in range(0, width, piece)]
     return tiles
 
 
-def project_kernel(n, blocks, gated, waited, *refs):
+def project_kernel(n, blocks, gated, *refs):
     k = len(blocks)
-    refs = refs[waited:]
     tiles = tiles_of(blocks)
     if gated:
         gate_hbm, up_hbm, tokens_hbm, weight_ref, *refs = refs
@@ -62,10 +69,9 @@
         return copy
 
     def columns(i, c, width):
-        bits, halved, at, block, keep = blocks[i]
-        if halved:
-            side = side_of(me, bits[0])
-            at += (side if keep else 1 - side) * block
+        masks, at, block, keep = blocks[i]
+        side = side_of(n, masks)
+        at += (side if keep else 1 - side) * block
         return pl.ds(pl.multiple_of(at + c, 128), width)
 
     if gated:
@@ -91,7 +97,7 @@
         outs[i][:, c : c + width] = (product + jnp.where(owner == me, own, 0.0)).astype(BF16)
 
 
-def project(n, blocks, gated, ins, tokens, weight, after=()):
+def project(n, blocks, gated, ins, tokens, weight):
     depth = weight.shape[0]
     rows = tokens.shape[0] * n
     vmem, hbm = pl.BlockSpec(memory_space=pltpu.VMEM), pl.BlockSpec(memory_space=pl.ANY)
@@ -105,9 +111,9 @@
     pinned = [*(ins if gated else ()), tokens, weight]
     pinned = [pltpu.with_memory_space_constraint(x, pltpu.HBM) for x in pinned]
     return pl.pallas_call(
-        functools.partial(project_kernel, n, blocks, gated, len(after)),
+        functools.partial(project_kernel, n, blocks, gated),
         out_shape=shapes,
-        in_specs=[hbm] * len(after) + [hbm if gated else vmem] * len(ins) + [hbm, hbm],
+        in_specs=[hbm if gated else vmem] * len(ins) + [hbm, hbm],
         out_specs=[vmem] * len(shapes),
         scratch_shapes=scratch
         + [pltpu.VMEM((depth, w), BF16) for _, _, w in tiles]
@@ -118,18 +124,18 @@
             bytes_accessed=2 * depth * columns,
             transcendentals=0,
         ),
-    )(*after, *(() if gated else ins), *pinned)
-
-
-def norm_kernel(chunks, *refs):
+    )(*(() if gated else ins), *pinned)
+
+
+def norm_kernel(n, chunks, *refs):
     *pieces, gain_ref, residual_ref, rows_ref, scale_ref, scaled_ref = refs
     me = lax.axis_index("tensor")
     mine = pl.ds(pl.multiple_of(me * residual_ref.shape[0], 16), residual_ref.shape[0])
     squares, largest = 0.0, 0.0
     pieces = iter(pieces)
-    for bits, halved, at, width in chunks:
-        side = side_of(me, bits[0])
-        for first in (at + side * width, at + (1 - side) * width) if halved else (at,):
+    for masks, at, width in chunks:
+        side = side_of(n, masks)
+        for first in (at + side * width, at + (1 - side) * width):
             piece = next(pieces)
             cols = pl.ds(pl.multiple_of(first, 128), width)
             residual_ref[:, cols] = piece[mine, :]
@@ -143,11 +149,11 @@
     scale_ref[...] = (largest * lax.rsqrt(mean + 1e-05)).reshape(-1)
 
 
-def norm(rows, chunks, pieces, gain):
+def norm(n, rows, chunks, pieces, gain):
     count, width = pieces[0].shape[0], gain.shape[0]
     vmem = pl.BlockSpec(memory_space=pltpu.VMEM)
     return pl.pallas_call(
-        functools.partial(norm_kernel, chunks),
+        functools.partial(norm_kernel, n, chunks),
         out_shape=[
             jax.ShapeDtypeStruct((rows, width), BF16),
             jax.ShapeDtypeStruct((count, width), BF16),
@@ -160,43 +166,58 @@
     )(*pieces, gain.reshape(1, width))
 
 
-def body(n, tokens, gate_act, up_act, down_weight, norm_gain):
+def body(n, batches, tokens, gate_act, up_act, down_weight, norm_gain):
     chunks = chunks_of(n, down_weight.shape[1])
-    def swap(x, bit):
-        return lax.ppermute(x, "tensor", [(i, i ^ bit) for i in range(n)])
+
+    def swap(x, masks):
+        pairs = [
+            (d * n + t, d * n + (t ^ masks[d % 2])) for d in range(batches) for t in range(n)
+        ]
+        return lax.ppermute(x, ("dp", "tensor"), pairs)
 
     def add(a, b):
         return (a.astype(F32) + b.astype(F32)).astype(BF16)
 
-    made, arrived = {}, {}
-    for step, chosen in enumerate(PLAN):
-        ins = (hidden,) if step else (gate_act, up_act)
-        blocks = [(*chunks[i], keep) for i, keep in chosen]
-        after = [arrived[AFTER[step]]] if step in AFTER else []
-        outs = project(n, blocks, not step, ins, tokens, down_weight, after)
-        if not step:
-            *outs, hidden = outs
-        made.update(zip(chosen, outs))
-        for i, keep in chosen:
-            bits, halved, _, _ = chunks[i]
-            if not keep or not halved:
-                arrived[i] = swap(made[i, keep], bits[0])
+    stages = len(chunks[0][0][0]) + 1
+    made, arrivals, sums = {}, {}, {}
+
+    def run(step):
+        ins = (made["hidden"],) if step else (gate_act, up_act)
+        blocks = [(*chunks[i], keep) for i, keep in PLAN[step]]
+        return project(n, blocks, not step, ins, tokens, down_weight)
+
+    def block(i, keep):
+        if not made:
+            *outs, made["hidden"] = run(0)
+            made.update(zip(PLAN[0], outs))
+        if (i, keep) not in made:
+            step = [(i, keep) in chosen for chosen in PLAN].index(True)
+            made.update(zip(PLAN[step], run(step)))
+        return made[i, keep]
+
+    def arrived(i, stage):
+        if (i, stage) not in arrivals:
+            x = total(i, stage - 1) if stage else block(i, False)
+            masks = [[*masks, masks[0]][stage] for masks in chunks[i][0]]
+            arrivals[i, stage] = swap(x, masks)
+        return arrivals[i, stage]
+
+    def total(i, stage):
+        if (i, stage) not in sums:
+            other = arrived(i, stage)
+            sums[i, stage] = add(total(i, stage - 1) if stage else block(i, True), other)
+        return sums[i, stage]
 
     pieces = []
-    for i, (bits, halved, _, _) in enumerate(chunks):
-        total = add(made[i, True], arrived[i])
-        for bit in bits[1:]:
-            total = add(total, swap(total, bit))
-        pieces.append(total)
-        if halved:
-            pieces.append(swap(total, bits[0]))
-    return norm(tokens.shape[0], chunks, pieces, norm_gain)
+    for i in range(len(chunks)):
+        pieces += [total(i, stages - 2), arrived(i, stages - 1)]
+    return norm(n, tokens.shape[0], chunks, pieces, norm_gain)
 
 
 def solution(mesh):
     n = mesh.shape["tensor"]
     return jax.shard_map(
-        lambda *args: body(n, *args),
+        lambda *args: body(n, mesh.shape["dp"], *args),
         mesh=mesh,
         in_specs=(
             P(("dp", "tensor"), None),

time: 29.6 us -> 28.7 us (0.970)
  waiting for transfers between devices: 8.62 us -> 3.96 us
  starting transfers between devices: 12.6 us -> 16.5 us
    ppermute x6, waiting for transfers between devices: 8.62 us -> 3.96 us  [swap(): return lax.ppermute(x, ('dp', 'tensor'), pairs)]
    ppermute x6, starting transfers between devices: 12.6 us -> 16.5 us  [swap(): return lax.ppermute(x, ('dp', 'tensor'), pairs)]
where the time goes in v3:
time: 28.7 us; the launch traced here: 28.6 us
  starting transfers between devices  16.5 us (57%)
  Pallas kernels  7.26 us (25%)
  waiting for transfers between devices  3.96 us (14%)
  between operations  0.69 us (2%)
    ppermute x6, starting transfers between devices, swap(): return lax.ppermute(x, ('dp', 'tensor'), pairs)  16.5 us
    pallas_call x2, Pallas kernels, project(): pl.pallas_call(functools.partial(project_kernel, n, blocks, gated), out_s...  6.15 us
    ppermute x6, waiting for transfers between devices, swap(): return lax.ppermute(x, ('dp', 'tensor'), pairs)  3.96 us
    pallas_call x1, Pallas kernels, norm(): pl.pallas_call(functools.partial(norm_kernel, n, chunks), out_shape=[jax....  1.12 us
  transfers between devices with their start and end apart: 6, of which 4 were waited for; matrix products, arithmetic and copies ran while one was open for 0% of the time, Pallas kernels for 10%

profile of v3, /device:TPU:0, one launch (start us, length us, event | category | flops | bytes accessed | tf_op | source)
XLA Modules:
  0.0 28.6 jit_solution(6302726626556166547)
XLA Ops:
  0.6 0.0 copy-start
  0.6 3.2 %shard_map.76 = (bf16[64,1024]{1,0:T(8,128)(2,1)S(1)}, bf16[64,1024]{1,0:T(8,128)(2,1)S(1)}, bf16[64,1280]{1,0:T(8,128)(2,1)S(1)}) custom-call(bf16[64,1280]{1,0:T(8,128)(2,1)} %refs_0_.1, bf16[64,1280]{1,0:T(8,128)(2,1)} %refs_1_.2, bf16[16,4096]{1,0:T(8,128)(2,1)} %refs_1_.3, bf16[1280,4096]{1,0:T(8,128)(2,1)} %refs_2_.3), custom_call_target="tpu_custom_call" | custom-call | flops 335544320 | bytes 5242880 | tf_op jit(solution)/shard_map/pallas_call | solution.py:113
  3.8 4.1 %collective-permute-start = (bf16[64,1024]{1,0:T(8,128)(2,1)S(1)}, bf16[64,1024]{1,0:T(8,128)(2,1)S(1)}, u32[]{:S(2)}, u32[]{:S(2)}) collective-permute-start(bf16[64,1024]{1,0:T(8,128)(2,1)S(1)} %get-tuple-element.10), channel_id=1, source_target_pairs={{0,2},{1,3},{2,0},{3,1},{4,5},{5,4},{6,7},{7,6},{8,10},{9,11},{10,... | collective-permute-start | bytes 393224 | tf_op jit(solution)/shard_map/ppermute | solution.py:176
  7.9 1.6 %collective-permute-start.3 = (bf16[64,1024]{1,0:T(8,128)(2,1)S(1)}, bf16[64,1024]{1,0:T(8,128)(2,1)S(1)}, u32[]{:S(2)}, u32[]{:S(2)}) collective-permute-start(bf16[64,1024]{1,0:T(8,128)(2,1)S(1)} %get-tuple-element.12), channel_id=1, source_target_pairs={{0,1},{1,0},{2,3},{3,2},{4,5},{5,4},{6,7},{7,6},{8,9},{9,8},{10,11... | collective-permute-start | bytes 393224 | tf_op jit(solution)/shard_map/ppermute | solution.py:176
  9.5 3.0 %shard_map.77 = (bf16[64,1024]{1,0:T(8,128)(2,1)S(1)}, bf16[64,1024]{1,0:T(8,128)(2,1)S(1)}) custom-call(bf16[64,1280]{1,0:T(8,128)(2,1)S(1)} %get-tuple-element.8.refs_0_, bf16[16,4096]{1,0:T(8,128)(2,1)} %refs_1_.3, bf16[1280,4096]{1,0:T(8,128)(2,1)} %refs_2_.3), custom_call_target="tpu_custom_call" | custom-call | flops 335544320 | bytes 5242880 | tf_op jit(solution)/shard_map/pallas_call | solution.py:113
  12.5 0.0 collective-permute-done
  12.5 1.7 %collective-permute-start.1 = (bf16[64,1024]{1,0:T(8,128)(2,1)S(1)}, bf16[64,1024]{1,0:T(8,128)(2,1)S(1)}, u32[]{:S(2)}, u32[]{:S(2)}) collective-permute-start(bf16[64,1024]{1,0:T(8,128)(2,1)S(1)} %add_convert_fusion.3), channel_id=1, source_target_pairs={{0,1},{1,0},{2,3},{3,2},{4,6},{5,7},{6,4},{7,5},{8,9},{9,8},{10,11... | collective-permute-start | bytes 393224 | tf_op jit(solution)/shard_map/ppermute | solution.py:176
  14.3 0.0 collective-permute-done.3
  14.3 2.8 %collective-permute-start.4 = (bf16[64,1024]{1,0:T(8,128)(2,1)S(1)}, bf16[64,1024]{1,0:T(8,128)(2,1)S(1)}, u32[]{:S(2)}, u32[]{:S(2)}) collective-permute-start(bf16[64,1024]{1,0:T(8,128)(2,1)S(1)} %add_convert_fusion.1), channel_id=1, source_target_pairs={{0,2},{1,3},{2,0},{3,1},{4,7},{5,6},{6,5},{7,4},{8,10},{9,11},{10,... | collective-permute-start | bytes 393224 | tf_op jit(solution)/shard_map/ppermute | solution.py:176
  17.1 0.5 %collective-permute-done.1 = bf16[64,1024]{1,0:T(8,128)(2,1)S(1)} collective-permute-done((bf16[64,1024]{1,0:T(8,128)(2,1)S(1)}, bf16[64,1024]{1,0:T(8,128)(2,1)S(1)}, u32[]{:S(2)}, u32[]{:S(2)}) %collective-permute-start.1) | collective-permute-done | bytes 131104 | tf_op jit(solution)/shard_map/ppermute | solution.py:176
  17.6 3.8 %collective-permute-start.2 = (bf16[64,1024]{1,0:T(8,128)(2,1)S(1)}, bf16[64,1024]{1,0:T(8,128)(2,1)S(1)}, u32[]{:S(2)}, u32[]{:S(2)}) collective-permute-start(bf16[64,1024]{1,0:T(8,128)(2,1)S(1)} %add_convert_fusion.2.refs_0_), channel_id=1, source_target_pairs={{0,2},{1,3},{2,0},{3,1},{4,5},{5,4},{6,7},{7,6},{8,10},{9,11},{10,... | collective-permute-start | bytes 393224 | tf_op jit(solution)/shard_map/ppermute | solution.py:176
  21.4 0.2 collective-permute-done.4
  21.7 2.5 %collective-permute-start.5 = (bf16[64,1024]{1,0:T(8,128)(2,1)S(1)}, bf16[64,1024]{1,0:T(8,128)(2,1)S(1)}, u32[]{:S(2)}, u32[]{:S(2)}) collective-permute-start(bf16[64,1024]{1,0:T(8,128)(2,1)S(1)} %add_convert_fusion.refs_2_), channel_id=1, source_target_pairs={{0,1},{1,0},{2,3},{3,2},{4,5},{5,4},{6,7},{7,6},{8,9},{9,8},{10,11... | collective-permute-start | bytes 393224 | tf_op jit(solution)/shard_map/ppermute | solution.py:176
  24.2 1.9 %collective-permute-done.2.refs_1_ = bf16[64,1024]{1,0:T(8,128)(2,1)S(1)} collective-permute-done((bf16[64,1024]{1,0:T(8,128)(2,1)S(1)}, bf16[64,1024]{1,0:T(8,128)(2,1)S(1)}, u32[]{:S(2)}, u32[]{:S(2)}) %collective-permute-start.2) | collective-permute-done | bytes 131104 | tf_op jit(solution)/shard_map/ppermute | solution.py:176
  26.1 1.4 %collective-permute-done.5.refs_3_ = bf16[64,1024]{1,0:T(8,128)(2,1)S(1)} collective-permute-done((bf16[64,1024]{1,0:T(8,128)(2,1)S(1)}, bf16[64,1024]{1,0:T(8,128)(2,1)S(1)}, u32[]{:S(2)}, u32[]{:S(2)}) %collective-permute-start.5) | collective-permute-done | bytes 131104 | tf_op jit(solution)/shard_map/ppermute | solution.py:176
  27.5 0.0 copy-done
  27.5 1.1 %shard_map.78 = (bf16[16,4096]{1,0:T(8,128)(2,1)}, bf16[64,4096]{1,0:T(8,128)(2,1)}, f32[64]{0:T(128)}) custom-call(bf16[64,1024]{1,0:T(8,128)(2,1)S(1)} %add_convert_fusion.2.refs_0_, bf16[64,1024]{1,0:T(8,128)(2,1)S(1)} %collective-permute-done.2.refs_1_, bf16[64,1024]{1,0:T(8,128)(2,1)S(1)} %add_convert_fusion.refs_2_, ...), custom_call_target="tpu_custom_call" | custom-call | tf_op jit(solution)/shard_map/pallas_call | solution.py:155
  (4 shorter events, 0.1 us)
Async XLA Ops:
  0.6 26.8 %copy-start = (f32[4096]{0:T(1024)S(1)}, f32[4096]{0:T(1024)}, u32[]{:S(2)}) copy-start(f32[4096]{0:T(1024)} %param.9) | copy-start | bytes 49156
  3.8 8.7 %collective-permute-start = (bf16[64,1024]{1,0:T(8,128)(2,1)S(1)}, bf16[64,1024]{1,0:T(8,128)(2,1)S(1)}, u32[]{:S(2)}, u32[]{:S(2)}) collective-permute-start(bf16[64,1024]{1,0:T(8,128)(2,1)S(1)} %get-tuple-element.10), channel_id=1, source_target_pairs={{0,2},{1,3},{2,0},{3,1},{4,5},{5,4},{6,7},{7,6},{8,10},{9,11},{10,... | collective-permute-start | bytes 393224 | tf_op jit(solution)/shard_map/ppermute | solution.py:176
  7.9 6.4 %collective-permute-start.3 = (bf16[64,1024]{1,0:T(8,128)(2,1)S(1)}, bf16[64,1024]{1,0:T(8,128)(2,1)S(1)}, u32[]{:S(2)}, u32[]{:S(2)}) collective-permute-start(bf16[64,1024]{1,0:T(8,128)(2,1)S(1)} %get-tuple-element.12), channel_id=1, source_target_pairs={{0,1},{1,0},{2,3},{3,2},{4,5},{5,4},{6,7},{7,6},{8,9},{9,8},{10,11... | collective-permute-start | bytes 393224 | tf_op jit(solution)/shard_map/ppermute | solution.py:176
  12.5 5.0 %collective-permute-start.1 = (bf16[64,1024]{1,0:T(8,128)(2,1)S(1)}, bf16[64,1024]{1,0:T(8,128)(2,1)S(1)}, u32[]{:S(2)}, u32[]{:S(2)}) collective-permute-start(bf16[64,1024]{1,0:T(8,128)(2,1)S(1)} %add_convert_fusion.3), channel_id=1, source_target_pairs={{0,1},{1,0},{2,3},{3,2},{4,6},{5,7},{6,4},{7,5},{8,9},{9,8},{10,11... | collective-permute-start | bytes 393224 | tf_op jit(solution)/shard_map/ppermute | solution.py:176
  14.3 7.3 %collective-permute-start.4 = (bf16[64,1024]{1,0:T(8,128)(2,1)S(1)}, bf16[64,1024]{1,0:T(8,128)(2,1)S(1)}, u32[]{:S(2)}, u32[]{:S(2)}) collective-permute-start(bf16[64,1024]{1,0:T(8,128)(2,1)S(1)} %add_convert_fusion.1), channel_id=1, source_target_pairs={{0,2},{1,3},{2,0},{3,1},{4,7},{5,6},{6,5},{7,4},{8,10},{9,11},{10,... | collective-permute-start | bytes 393224 | tf_op jit(solution)/shard_map/ppermute | solution.py:176
  17.6 8.5 %collective-permute-start.2 = (bf16[64,1024]{1,0:T(8,128)(2,1)S(1)}, bf16[64,1024]{1,0:T(8,128)(2,1)S(1)}, u32[]{:S(2)}, u32[]{:S(2)}) collective-permute-start(bf16[64,1024]{1,0:T(8,128)(2,1)S(1)} %add_convert_fusion.2.refs_0_), channel_id=1, source_target_pairs={{0,2},{1,3},{2,0},{3,1},{4,5},{5,4},{6,7},{7,6},{8,10},{9,11},{10,... | collective-permute-start | bytes 393224 | tf_op jit(solution)/shard_map/ppermute | solution.py:176
  21.7 5.8 %collective-permute-start.5 = (bf16[64,1024]{1,0:T(8,128)(2,1)S(1)}, bf16[64,1024]{1,0:T(8,128)(2,1)S(1)}, u32[]{:S(2)}, u32[]{:S(2)}) collective-permute-start(bf16[64,1024]{1,0:T(8,128)(2,1)S(1)} %add_convert_fusion.refs_2_), channel_id=1, source_target_pairs={{0,1},{1,0},{2,3},{3,2},{4,5},{5,4},{6,7},{7,6},{8,9},{9,8},{10,11... | collective-permute-start | bytes 393224 | tf_op jit(solution)/shard_map/ppermute | solution.py:176

commit v4 on v3

--- a/solution.py
+++ b/solution.py
@@ -8,7 +8,7 @@
 from jax.sharding import PartitionSpec as P
 
 F32, BF16 = jnp.float32, jnp.bfloat16
-TILE = 512
+TILES = {True: 512, False: 1024}
 CHUNKS = ((8, ((2, 1), (1, 2))), (8, ((1, 2), (1, 3))))
 PLAN = (((0, False), (1, False)), ((0, True), (1, True)))
 VMEM_LIMIT = 32 * 1024 * 1024
@@ -41,10 +41,10 @@
     return jnp.where(core == 0, sides[0], sides[1])
 
 
-def tiles_of(blocks):
+def tiles_of(blocks, most):
     tiles = []
     for i, (_, _, width, _) in enumerate(blocks):
-        count = -(-width // TILE)
+        count = -(-width // most)
         piece = -(-width // count // 128) * 128
         tiles += [(i, c, min(piece, width - c)) for c in range(0, width, piece)]
     return tiles
@@ -52,7 +52,7 @@
 
 def project_kernel(n, blocks, gated, *refs):
     k = len(blocks)
-    tiles = tiles_of(blocks)
+    tiles = tiles_of(blocks, TILES[gated])
     if gated:
         gate_hbm, up_hbm, tokens_hbm, weight_ref, *refs = refs
     else:
@@ -107,7 +107,7 @@
         shapes.append(jax.ShapeDtypeStruct((rows, depth), BF16))
         scratch = [pltpu.VMEM((rows, depth), BF16)] * 2 + scratch
     columns = sum(w for *_, w, _ in blocks)
-    tiles = tiles_of(blocks)
+    tiles = tiles_of(blocks, TILES[gated])
     pinned = [*(ins if gated else ()), tokens, weight]
     pinned = [pltpu.with_memory_space_constraint(x, pltpu.HBM) for x in pinned]
     return pl.pallas_call(

time: 28.7 us -> 28.7 us (level)
  starting transfers between devices: 16.5 us -> 16.1 us
    ppermute x6, starting transfers between devices: 16.5 us -> 16.1 us  [swap(): return lax.ppermute(x, ('dp', 'tensor'), pairs)]
  transfers between devices with their start and end apart: 6 -> 6, of which waited for: 4 -> 4; matrix products, arithmetic and copies ran while one was open for 0% -> 0% of each run, Pallas kernels for 10% -> 11%
where the time goes in v4:
time: 28.7 us; the launch traced here: 28.6 us
  starting transfers between devices  16.1 us (56%)
  Pallas kernels  7.48 us (26%)
  waiting for transfers between devices  4.2 us (15%)
  between operations  0.69 us (2%)
    ppermute x6, starting transfers between devices, swap(): return lax.ppermute(x, ('dp', 'tensor'), pairs)  16.1 us
    pallas_call x2, Pallas kernels, project(): pl.pallas_call(functools.partial(project_kernel, n, blocks, gated), out_s...  6.37 us
    ppermute x6, waiting for transfers between devices, swap(): return lax.ppermute(x, ('dp', 'tensor'), pairs)  4.2 us
    pallas_call x1, Pallas kernels, norm(): pl.pallas_call(functools.partial(norm_kernel, n, chunks), out_shape=[jax....  1.12 us
  transfers between devices with their start and end apart: 6, of which 4 were waited for; matrix products, arithmetic and copies ran while one was open for 0% of the time, Pallas kernels for 11%

profile of v4, /device:TPU:0, one launch (start us, length us, event | category | flops | bytes accessed | tf_op | source)
XLA Modules:
  0.0 28.6 jit_solution(13764374141446193436)
XLA Ops:
  0.6 0.0 copy-start
  0.6 3.2 %shard_map.76 = (bf16[64,1024]{1,0:T(8,128)(2,1)S(1)}, bf16[64,1024]{1,0:T(8,128)(2,1)S(1)}, bf16[64,1280]{1,0:T(8,128)(2,1)S(1)}) custom-call(bf16[64,1280]{1,0:T(8,128)(2,1)} %refs_0_.1, bf16[64,1280]{1,0:T(8,128)(2,1)} %refs_1_.2, bf16[16,4096]{1,0:T(8,128)(2,1)} %refs_1_.3, bf16[1280,4096]{1,0:T(8,128)(2,1)} %refs_2_.3), custom_call_target="tpu_custom_call" | custom-call | flops 335544320 | bytes 5242880 | tf_op jit(solution)/shard_map/pallas_call | solution.py:113
  3.8 4.1 %collective-permute-start = (bf16[64,1024]{1,0:T(8,128)(2,1)S(1)}, bf16[64,1024]{1,0:T(8,128)(2,1)S(1)}, u32[]{:S(2)}, u32[]{:S(2)}) collective-permute-start(bf16[64,1024]{1,0:T(8,128)(2,1)S(1)} %get-tuple-element.10), channel_id=1, source_target_pairs={{0,2},{1,3},{2,0},{3,1},{4,5},{5,4},{6,7},{7,6},{8,10},{9,11},{10,... | collective-permute-start | bytes 393224 | tf_op jit(solution)/shard_map/ppermute | solution.py:176
  7.9 1.6 %collective-permute-start.3 = (bf16[64,1024]{1,0:T(8,128)(2,1)S(1)}, bf16[64,1024]{1,0:T(8,128)(2,1)S(1)}, u32[]{:S(2)}, u32[]{:S(2)}) collective-permute-start(bf16[64,1024]{1,0:T(8,128)(2,1)S(1)} %get-tuple-element.12), channel_id=1, source_target_pairs={{0,1},{1,0},{2,3},{3,2},{4,5},{5,4},{6,7},{7,6},{8,9},{9,8},{10,11... | collective-permute-start | bytes 393224 | tf_op jit(solution)/shard_map/ppermute | solution.py:176
  9.5 3.2 %shard_map.77 = (bf16[64,1024]{1,0:T(8,128)(2,1)S(1)}, bf16[64,1024]{1,0:T(8,128)(2,1)S(1)}) custom-call(bf16[64,1280]{1,0:T(8,128)(2,1)S(1)} %get-tuple-element.8.refs_0_, bf16[16,4096]{1,0:T(8,128)(2,1)} %refs_1_.3, bf16[1280,4096]{1,0:T(8,128)(2,1)} %refs_2_.3), custom_call_target="tpu_custom_call" | custom-call | flops 335544320 | bytes 5242880 | tf_op jit(solution)/shard_map/pallas_call | solution.py:113
  12.7 0.0 collective-permute-done
  12.8 1.5 %collective-permute-start.1 = (bf16[64,1024]{1,0:T(8,128)(2,1)S(1)}, bf16[64,1024]{1,0:T(8,128)(2,1)S(1)}, u32[]{:S(2)}, u32[]{:S(2)}) collective-permute-start(bf16[64,1024]{1,0:T(8,128)(2,1)S(1)} %add_convert_fusion.3), channel_id=1, source_target_pairs={{0,1},{1,0},{2,3},{3,2},{4,6},{5,7},{6,4},{7,5},{8,9},{9,8},{10,11... | collective-permute-start | bytes 393224 | tf_op jit(solution)/shard_map/ppermute | solution.py:176
  14.3 0.0 collective-permute-done.3
  14.3 2.7 %collective-permute-start.4 = (bf16[64,1024]{1,0:T(8,128)(2,1)S(1)}, bf16[64,1024]{1,0:T(8,128)(2,1)S(1)}, u32[]{:S(2)}, u32[]{:S(2)}) collective-permute-start(bf16[64,1024]{1,0:T(8,128)(2,1)S(1)} %add_convert_fusion.1), channel_id=1, source_target_pairs={{0,2},{1,3},{2,0},{3,1},{4,7},{5,6},{6,5},{7,4},{8,10},{9,11},{10,... | collective-permute-start | bytes 393224 | tf_op jit(solution)/shard_map/ppermute | solution.py:176
  17.1 0.7 %collective-permute-done.1 = bf16[64,1024]{1,0:T(8,128)(2,1)S(1)} collective-permute-done((bf16[64,1024]{1,0:T(8,128)(2,1)S(1)}, bf16[64,1024]{1,0:T(8,128)(2,1)S(1)}, u32[]{:S(2)}, u32[]{:S(2)}) %collective-permute-start.1) | collective-permute-done | bytes 131104 | tf_op jit(solution)/shard_map/ppermute | solution.py:176
  17.8 3.6 %collective-permute-start.2 = (bf16[64,1024]{1,0:T(8,128)(2,1)S(1)}, bf16[64,1024]{1,0:T(8,128)(2,1)S(1)}, u32[]{:S(2)}, u32[]{:S(2)}) collective-permute-start(bf16[64,1024]{1,0:T(8,128)(2,1)S(1)} %add_convert_fusion.2.refs_0_), channel_id=1, source_target_pairs={{0,2},{1,3},{2,0},{3,1},{4,5},{5,4},{6,7},{7,6},{8,10},{9,11},{10,... | collective-permute-start | bytes 393224 | tf_op jit(solution)/shard_map/ppermute | solution.py:176
  21.4 0.2 collective-permute-done.4
  21.7 2.5 %collective-permute-start.5 = (bf16[64,1024]{1,0:T(8,128)(2,1)S(1)}, bf16[64,1024]{1,0:T(8,128)(2,1)S(1)}, u32[]{:S(2)}, u32[]{:S(2)}) collective-permute-start(bf16[64,1024]{1,0:T(8,128)(2,1)S(1)} %add_convert_fusion.refs_2_), channel_id=1, source_target_pairs={{0,1},{1,0},{2,3},{3,2},{4,5},{5,4},{6,7},{7,6},{8,9},{9,8},{10,11... | collective-permute-start | bytes 393224 | tf_op jit(solution)/shard_map/ppermute | solution.py:176
  24.2 1.9 %collective-permute-done.2.refs_1_ = bf16[64,1024]{1,0:T(8,128)(2,1)S(1)} collective-permute-done((bf16[64,1024]{1,0:T(8,128)(2,1)S(1)}, bf16[64,1024]{1,0:T(8,128)(2,1)S(1)}, u32[]{:S(2)}, u32[]{:S(2)}) %collective-permute-start.2) | collective-permute-done | bytes 131104 | tf_op jit(solution)/shard_map/ppermute | solution.py:176
  26.1 1.4 %collective-permute-done.5.refs_3_ = bf16[64,1024]{1,0:T(8,128)(2,1)S(1)} collective-permute-done((bf16[64,1024]{1,0:T(8,128)(2,1)S(1)}, bf16[64,1024]{1,0:T(8,128)(2,1)S(1)}, u32[]{:S(2)}, u32[]{:S(2)}) %collective-permute-start.5) | collective-permute-done | bytes 131104 | tf_op jit(solution)/shard_map/ppermute | solution.py:176
  27.5 0.0 copy-done
  27.5 1.1 %shard_map.78 = (bf16[16,4096]{1,0:T(8,128)(2,1)}, bf16[64,4096]{1,0:T(8,128)(2,1)}, f32[64]{0:T(128)}) custom-call(bf16[64,1024]{1,0:T(8,128)(2,1)S(1)} %add_convert_fusion.2.refs_0_, bf16[64,1024]{1,0:T(8,128)(2,1)S(1)} %collective-permute-done.2.refs_1_, bf16[64,1024]{1,0:T(8,128)(2,1)S(1)} %add_convert_fusion.refs_2_, ...), custom_call_target="tpu_custom_call" | custom-call | tf_op jit(solution)/shard_map/pallas_call | solution.py:155
  (4 shorter events, 0.1 us)
Async XLA Ops:
  0.6 26.8 %copy-start = (f32[4096]{0:T(1024)S(1)}, f32[4096]{0:T(1024)}, u32[]{:S(2)}) copy-start(f32[4096]{0:T(1024)} %param.9) | copy-start | bytes 49156
  3.8 8.9 %collective-permute-start = (bf16[64,1024]{1,0:T(8,128)(2,1)S(1)}, bf16[64,1024]{1,0:T(8,128)(2,1)S(1)}, u32[]{:S(2)}, u32[]{:S(2)}) collective-permute-start(bf16[64,1024]{1,0:T(8,128)(2,1)S(1)} %get-tuple-element.10), channel_id=1, source_target_pairs={{0,2},{1,3},{2,0},{3,1},{4,5},{5,4},{6,7},{7,6},{8,10},{9,11},{10,... | collective-permute-start | bytes 393224 | tf_op jit(solution)/shard_map/ppermute | solution.py:176
  7.9 6.4 %collective-permute-start.3 = (bf16[64,1024]{1,0:T(8,128)(2,1)S(1)}, bf16[64,1024]{1,0:T(8,128)(2,1)S(1)}, u32[]{:S(2)}, u32[]{:S(2)}) collective-permute-start(bf16[64,1024]{1,0:T(8,128)(2,1)S(1)} %get-tuple-element.12), channel_id=1, source_target_pairs={{0,1},{1,0},{2,3},{3,2},{4,5},{5,4},{6,7},{7,6},{8,9},{9,8},{10,11... | collective-permute-start | bytes 393224 | tf_op jit(solution)/shard_map/ppermute | solution.py:176
  12.8 5.0 %collective-permute-start.1 = (bf16[64,1024]{1,0:T(8,128)(2,1)S(1)}, bf16[64,1024]{1,0:T(8,128)(2,1)S(1)}, u32[]{:S(2)}, u32[]{:S(2)}) collective-permute-start(bf16[64,1024]{1,0:T(8,128)(2,1)S(1)} %add_convert_fusion.3), channel_id=1, source_target_pairs={{0,1},{1,0},{2,3},{3,2},{4,6},{5,7},{6,4},{7,5},{8,9},{9,8},{10,11... | collective-permute-start | bytes 393224 | tf_op jit(solution)/shard_map/ppermute | solution.py:176
  14.3 7.3 %collective-permute-start.4 = (bf16[64,1024]{1,0:T(8,128)(2,1)S(1)}, bf16[64,1024]{1,0:T(8,128)(2,1)S(1)}, u32[]{:S(2)}, u32[]{:S(2)}) collective-permute-start(bf16[64,1024]{1,0:T(8,128)(2,1)S(1)} %add_convert_fusion.1), channel_id=1, source_target_pairs={{0,2},{1,3},{2,0},{3,1},{4,7},{5,6},{6,5},{7,4},{8,10},{9,11},{10,... | collective-permute-start | bytes 393224 | tf_op jit(solution)/shard_map/ppermute | solution.py:176
  17.8 8.3 %collective-permute-start.2 = (bf16[64,1024]{1,0:T(8,128)(2,1)S(1)}, bf16[64,1024]{1,0:T(8,128)(2,1)S(1)}, u32[]{:S(2)}, u32[]{:S(2)}) collective-permute-start(bf16[64,1024]{1,0:T(8,128)(2,1)S(1)} %add_convert_fusion.2.refs_0_), channel_id=1, source_target_pairs={{0,2},{1,3},{2,0},{3,1},{4,5},{5,4},{6,7},{7,6},{8,10},{9,11},{10,... | collective-permute-start | bytes 393224 | tf_op jit(solution)/shard_map/ppermute | solution.py:176
  21.7 5.8 %collective-permute-start.5 = (bf16[64,1024]{1,0:T(8,128)(2,1)S(1)}, bf16[64,1024]{1,0:T(8,128)(2,1)S(1)}, u32[]{:S(2)}, u32[]{:S(2)}) collective-permute-start(bf16[64,1024]{1,0:T(8,128)(2,1)S(1)} %add_convert_fusion.refs_2_), channel_id=1, source_target_pairs={{0,1},{1,0},{2,3},{3,2},{4,5},{5,4},{6,7},{7,6},{8,9},{9,8},{10,11... | collective-permute-start | bytes 393224 | tf_op jit(solution)/shard_map/ppermute | solution.py:176
